TPU v7x, 256 devices: a whole 4x4x8 slice. The times are simulated.
256 devices in a mesh: pool: 32 (over z, y_lo, core), pw: 8 (over x, y_hi).
Axes of the slice: x: 4, y: 4 (y_hi: 2, y_lo: 2; y = y_hi * 2 + y_lo), z: 8, core: 2. Of those that a mesh axis runs over, the one named last changes fastest.
Arguments:
- wave_block: bfloat16 [32, 2, 8, 61440], P('pool', None, None, 'pw'), may hold values from -6 to 6
- occupied: bfloat16 [32, 2, 64, 61440], P('pool', None, None, 'pw'), may hold values from -0.0625 to 0.0625
- radial: bfloat16 [32, 9, 61440], P('pool', None, 'pw'), may hold values from -6 to 6
- k_points: float32 [32, 3], replicated, may hold values from -1 to 1
- g_vectors: float32 [3, 61440], P(None, 'pw'), may hold values from -6 to 6
- structure: bfloat16 [2, 216, 61440], P(None, None, 'pw'), may hold values from -1 to 1, as said below
- positions: float32 [3, 216], replicated, may hold values from 0 to 4
- displacement: float32 [3, 216], replicated, may hold values from -6 to 6
- coupling: float32 [2, 9, 9], replicated, may hold values from -2 to 2
- atom_kind: int32 [216], replicated, may hold values from 0 to 1
- kq_index: int32 [32], replicated, may hold values from 0 to 31, as said below
- occ_count: int32 [32], replicated, may hold values from 32 to 64, as said below
Outputs:
- response: bfloat16 [32, 2, 8, 61440], P('pool', None, None, 'pw')
Inputs may be any that keep to these rules, and one draw needn't show every extreme that they name: structure[0] and structure[1] are the cosine and sine of one angle. kq_index[k] = (k + s) mod 32 for one s, the same for every k, where s is a power of two below 32. `occ_count`: some k-point has exactly 64 occupied bands.
All inputs are finite; a program needn't handle non-finite values.
Results may differ from a plain program's by a relative error of at most 0.024.
Values may be sent and summed in bfloat16 or wider, within the bound.
A program may use at most 64 MiB of HBM per device.

v0:
```python
import functools
import math

import jax
import jax.numpy as jnp
from jax import lax
from jax.experimental import pallas as pl
from jax.experimental.pallas import tpu as pltpu
from jax.sharding import PartitionSpec as P

ATOMS = 216
TYPES = 9
PW = 61440
GROUP = 4
GROUPS = 2
ROWS = 4 * TYPES
PAD = 40
HALF = 128
MESH = pl.DeviceIdType.MESH
F32 = jnp.float32
BF16 = jnp.bfloat16


def dot_nt(a, b):
    return lax.dot_general(a, b, (((1,), (1,)), ((), ())), preferred_element_type=F32)


def dot_nn(a, b):
    return lax.dot_general(a, b, (((1,), (0,)), ((), ())), preferred_element_type=F32)


def kernel(
    wave_in,
    occ_in,
    radial_in,
    kpts_in,
    gvec_in,
    struct_in,
    pos_in,
    disp_in,
    coupling_in,
    kind_in,
    index_in,
    count_in,
    out_ref,
    wave,
    occ,
    radial,
    kpts,
    gvec,
    struct,
    pos_raw,
    disp_raw,
    coupling,
    kind_raw,
    index,
    count,
    weights,
    moments,
    acc,
    tables,
    kinds,
    couple,
    coef,
    deriv,
    vert,
    vert_full,
    vert_op,
    applied,
    part_send,
    part_recv,
    vert_send,
    candidates,
    gathered,
    corr_send,
    corr_recv,
    load_sem,
    struct_sem,
    part_ssem,
    part_rsem,
    shift_ssem,
    shift_rsem,
    gather_ssem,
    gather_rsem,
    corr_ssem,
    corr_rsem,
):
    pools = lax.axis_size("pool")
    n = lax.axis_size("pw")
    pool = lax.axis_index("pool")
    me = lax.axis_index("pw")
    planes = wave.shape[-1]
    levels = shift_rsem.shape[1]
    halves = (slice(0, HALF), slice(HALF, ATOMS))

    def load(pairs, first):
        copies = []
        for i, (src, dst) in enumerate(pairs):
            copy = pltpu.make_async_copy(src, dst, load_sem.at[first + i])
            copy.start()
            copies.append(copy)
        return copies

    early = load(
        (
            (kpts_in, kpts),
            (radial_in.at[0], radial),
            (gvec_in, gvec),
            (wave_in.at[0], wave),
        ),
        0,
    )
    struct_copies = []
    for i, (start, width) in enumerate(struct_spans(planes)):
        span = pl.ds(start, width)
        copy = pltpu.make_async_copy(
            struct_in.at[:, :, span], struct.at[:, :, span], struct_sem.at[i]
        )
        copy.start()
        struct_copies.append((span, copy))
    late = load(
        (
            (pos_in, pos_raw),
            (disp_in, disp_raw),
            (coupling_in, coupling),
            (kind_in, kind_raw),
            (index_in, index),
            (count_in, count),
            (occ_in.at[0], occ),
        ),
        4,
    )

    barrier = pltpu.get_barrier_semaphore()
    for j in range(1, n):
        pl.semaphore_signal(
            barrier, inc=1, device_id={"pw": lax.rem(me + j, n)}, device_id_type=MESH
        )
    offsets = []
    for level in range(levels):
        offsets += [o for o in (1 << level, pools - (1 << level)) if o not in offsets]
    for offset in offsets:
        pl.semaphore_signal(
            barrier, inc=1, device_id={"pool": lax.rem(pool + offset, pools)}, device_id_type=MESH
        )

    for copy in early:
        copy.wait()
    pool_lane = lax.broadcasted_iota(jnp.int32, (1, pools), 1)

    def pick(values, where):
        return jnp.sum(jnp.where(where, values, jnp.zeros_like(values)), axis=1, keepdims=True)

    here = pick(kpts[...], pool_lane == pool)
    rad = radial[...].astype(F32)
    weights[0:TYPES, :] = rad
    for c in range(3):
        weights[TYPES * (c + 1) : TYPES * (c + 2), :] = rad * (gvec[c : c + 1, :] + here[c : c + 1, :])
    acc[...] = jnp.zeros_like(acc)

    def fill_moments(group, span):
        rows = slice(GROUP * group, GROUP * (group + 1))
        held = jnp.concatenate(
            [wave[0, :, span].astype(F32)[rows], wave[1, :, span].astype(F32)[rows]], 0
        )
        for i in range(ROWS // 2):
            upper = weights[2 * i : 2 * i + 1, span] * held
            lower = weights[2 * i + 1 : 2 * i + 2, span] * held
            moments[group, 16 * i : 16 * i + 16, span] = jnp.concatenate([upper, lower], 0).astype(BF16)

    def send_parts(group):
        for b in range(GROUP):
            for h in range(2):
                re_rows = pl.ds(b, PAD, stride=8)
                im_rows = pl.ds(GROUP + b, PAD, stride=8)
                raw_re = acc[0, h, re_rows, :] + acc[1, h, im_rows, :]
                raw_im = acc[0, h, im_rows, :] - acc[1, h, re_rows, :]
                part_send[group, 2 * b + h] = jnp.concatenate([raw_re, raw_im], 0).astype(BF16)
        sent = []
        for j in range(1, n):
            peer = lax.rem(me + j, n)
            copy = pltpu.make_async_remote_copy(
                src_ref=part_send.at[group, peer],
                dst_ref=part_recv.at[group, j],
                send_sem=part_ssem.at[group, j],
                recv_sem=part_rsem.at[group, j],
                device_id={"pw": peer},
                device_id_type=MESH,
            )
            copy.start()
            sent.append(copy)
        return sent

    for span, copy in struct_copies:
        fill_moments(0, span)
        copy.wait()
        for c in range(2):
            product = dot_nt(moments[0, :, span], struct[c, :, span])
            for h, cols in enumerate(halves):
                acc[c, h, 0 : 8 * ROWS, 0 : cols.stop - cols.start] += product[:, cols]
    pl.semaphore_wait(barrier, n - 1 + len(offsets))
    parts = [send_parts(0)]
    fill_moments(1, pl.ds(0, planes))
    for c in range(2):
        product = dot_nt(moments[1], struct[c])
        for h, cols in enumerate(halves):
            acc[c, h, 0 : 8 * ROWS, 0 : cols.stop - cols.start] = product[:, cols]
    parts.append(send_parts(1))

    for copy in late:
        copy.wait()
    half = lax.rem(me, 2)
    lanes = pl.ds(pl.multiple_of(half * HALF, HALF), HALF)
    tables[...] = jnp.zeros_like(tables)
    tables[0:3, 0:ATOMS] = pos_raw[...]
    tables[3:6, 0:ATOMS] = disp_raw[...]
    kinds[...] = jnp.zeros_like(kinds)
    kinds[0:1, 0:ATOMS] = kind_raw[...]
    target = pick(index[...], pool_lane == pool)
    there = pick(kpts[...], pool_lane == target)
    distance = lax.rem(target - pool + pools, pools)

    def phase(point):
        angle = (
            point[0:1, :] * tables[0:1, lanes]
            + point[1:2, :] * tables[1:2, lanes]
            + point[2:3, :] * tables[2:3, lanes]
        )
        return jnp.cos(angle), jnp.sin(angle)

    cos_here, sin_here = phase(here)
    cos_next, sin_next = phase(there)
    disp = [tables[3 + c : 4 + c, lanes] for c in range(3)]
    second = jnp.broadcast_to(kinds[0:1, lanes], (TYPES, HALF)) == 1
    first_table = coupling[:, 0, :]
    second_table = coupling[:, 1, :]
    for u in range(TYPES):
        first_col = jnp.broadcast_to(first_table[:, u : u + 1], (TYPES, HALF))
        second_col = jnp.broadcast_to(second_table[:, u : u + 1], (TYPES, HALF))
        couple[u] = jnp.where(second, second_col, first_col)
    vert[...] = jnp.zeros_like(vert)

    def send_vertex(group):
        total = part_send[group, me].astype(F32)
        for j in range(1, n):
            total += part_recv[group, j].astype(F32)
        scale = 1.0 / math.sqrt(PW)
        coef[0] = (cos_here * total[0:PAD] - sin_here * total[PAD:]) * scale
        coef[1] = (cos_here * total[PAD:] + sin_here * total[0:PAD]) * scale

        def moved(part):
            found = None
            for c in range(3):
                term = disp[c] * coef[part, TYPES * (c + 1) : TYPES * (c + 2), :]
                found = term if found is None else found + term
            return found

        deriv[0, 0:TYPES, :] = -moved(1)
        deriv[1, 0:TYPES, :] = moved(0)

        def coupled(source, part):
            found = None
            for u in range(TYPES):
                term = couple[u] * source[part, u : u + 1, :]
                found = term if found is None else found + term
            return found

        zc_re, zc_im = coupled(coef, 0), coupled(coef, 1)
        pieces = [(coupled(deriv, 0), coupled(deriv, 1))]
        pieces += [(disp[c] * zc_im, -disp[c] * zc_re) for c in range(3)]
        shrink = 1.0 / math.sqrt(4 * TYPES * ATOMS)
        for m, (re, im) in enumerate(pieces):
            vert[TYPES * m : TYPES * (m + 1), :] = (cos_next * re + sin_next * im) * shrink
            vert[PAD + TYPES * m : PAD + TYPES * (m + 1), :] = (cos_next * im - sin_next * re) * shrink
        vert_send[group] = vert[...].astype(BF16)
        sent = []
        for level in range(levels):
            copy = pltpu.make_async_remote_copy(
                src_ref=vert_send.at[group],
                dst_ref=candidates.at[group, level],
                send_sem=shift_ssem.at[group, level],
                recv_sem=shift_rsem.at[group, level],
                device_id={"pool": lax.rem(pool + (1 << level), pools)},
                device_id_type=MESH,
            )
            copy.start()
            sent.append(copy)
        return sent

    def pass_vertex(group):
        chosen = jnp.zeros((2 * PAD, HALF), F32)
        for level in range(levels):
            chosen = jnp.where(
                distance == (1 << level), candidates[group, level].astype(F32), chosen
            )
        gathered[group, me] = chosen.astype(BF16)
        sent = []
        for j in range(1, n):
            copy = pltpu.make_async_remote_copy(
                src_ref=gathered.at[group, me],
                dst_ref=gathered.at[group, me],
                send_sem=gather_ssem.at[group, j],
                recv_sem=gather_rsem.at[group, j],
                device_id={"pw": lax.rem(me + j, n)},
                device_id_type=MESH,
            )
            copy.start()
            sent.append(copy)
        return sent

    def apply_vertex(group):
        for b in range(GROUP):
            for h in range(2):
                piece = gathered[group, 2 * b + h].astype(F32)
                re_rows = pl.ds(b, PAD, stride=8)
                im_rows = pl.ds(GROUP + b, PAD, stride=8)
                vert_full[0, h, re_rows, :] = piece[0:PAD]
                vert_full[0, h, im_rows, :] = piece[PAD:]
                vert_full[1, h, re_rows, :] = -piece[PAD:]
                vert_full[1, h, im_rows, :] = piece[0:PAD]
        for h, cols in enumerate(halves):
            width_of = cols.stop - cols.start
            vert_op[:, :, cols] = vert_full[:, h, 0 : 8 * ROWS, 0:width_of].astype(BF16)
        spread = dot_nn(vert_op[0], struct[0])
        spread += dot_nn(vert_op[1], struct[1])
        total = None
        for i in range(ROWS):
            term = weights[i : i + 1, :] * spread[8 * i : 8 * i + 8]
            total = term if total is None else total + term
        rounded = total.astype(BF16).astype(F32)
        applied[GROUP * group : GROUP * (group + 1), :] = rounded[0:GROUP]
        applied[8 + GROUP * group : 8 + GROUP * (group + 1), :] = rounded[GROUP:]

    shifts = []
    for group in range(GROUPS):
        for copy in parts[group]:
            copy.wait_recv()
        shifts.append(send_vertex(group))
    passes = []
    for group in range(GROUPS):
        for copy in shifts[group]:
            copy.wait_recv()
        passes.append(pass_vertex(group))
    for group in range(GROUPS):
        for copy in passes[group]:
            copy.wait_recv()
        apply_vertex(group)

    occ_rows = occ.shape[1]
    corr_send[...] = dot_nt(applied[...].astype(BF16), occ[...].reshape(2 * occ_rows, planes))
    corrs = []
    for j in range(1, n):
        copy = pltpu.make_async_remote_copy(
            src_ref=corr_send,
            dst_ref=corr_recv.at[j],
            send_sem=corr_ssem.at[j],
            recv_sem=corr_rsem.at[j],
            device_id={"pw": lax.rem(me + j, n)},
            device_id_type=MESH,
        )
        copy.start()
        corrs.append(copy)
    live = pick(count[...], pool_lane == pool)
    for copy in corrs:
        copy.wait_recv()
    total = corr_send[...]
    for j in range(1, n):
        total += corr_recv[j]
    row = lax.broadcasted_iota(jnp.int32, total.shape, 0)
    lane = lax.broadcasted_iota(jnp.int32, total.shape, 1)
    swapped = pltpu.roll(jnp.concatenate([total[8:], total[:8]], 0), occ_rows, 1)
    same = (row >= 8) == (lane >= occ_rows)
    combined = jnp.where(same, total + swapped, total - swapped)
    state = jnp.where(lane >= occ_rows, lane - occ_rows, lane)
    kept = jnp.where(state < live, combined, 0.0).astype(BF16)
    removed = dot_nn(kept, occ[...].reshape(2 * occ_rows, planes))
    response = (applied[...] - removed).astype(BF16)
    out_ref[0, 0] = response[:8]
    out_ref[0, 1] = response[8:]
    for sent in parts + shifts + passes + [corrs]:
        for copy in sent:
            copy.wait_send()


def struct_spans(planes):
    unit = planes // 20
    return ((0, 4 * unit), (4 * unit, 6 * unit), (10 * unit, 10 * unit))


def perturb(operands, pools, n):
    wave, occ = operands[0], operands[1]
    planes = wave.shape[-1]
    occ_rows = occ.shape[2]
    levels = (pools - 1).bit_length()
    vmem, dma = pltpu.VMEM, pltpu.SemaphoreType.DMA
    scratch = [
        vmem((2, 8, planes), BF16),
        vmem((2, occ_rows, planes), BF16),
        vmem((TYPES, planes), BF16),
        vmem((3, pools), F32),
        vmem((3, planes), F32),
        vmem((2, ATOMS, planes), BF16),
        vmem((3, ATOMS), F32),
        vmem((3, ATOMS), F32),
        vmem((TYPES, 2, TYPES), F32),
        vmem((1, ATOMS), jnp.int32),
        vmem((1, pools), jnp.int32),
        vmem((1, pools), jnp.int32),
        vmem((PAD, planes), F32),
        vmem((GROUPS, 8 * ROWS, planes), BF16),
        vmem((2, 2, 8 * PAD, HALF), F32),
        vmem((8, 2 * HALF), F32),
        vmem((8, 2 * HALF), jnp.int32),
        vmem((TYPES, TYPES, HALF), F32),
        vmem((2, PAD, HALF), F32),
        vmem((2, 16, HALF), F32),
        vmem((2 * PAD, HALF), F32),
        vmem((2, 2, 8 * PAD, HALF), F32),
        vmem((2, 8 * ROWS, ATOMS), BF16),
        vmem((16, planes), F32),
        vmem((GROUPS, n, 2 * PAD, HALF), BF16),
        vmem((GROUPS, n, 2 * PAD, HALF), BF16),
        vmem((GROUPS, 2 * PAD, HALF), BF16),
        vmem((GROUPS, levels, 2 * PAD, HALF), BF16),
        vmem((GROUPS, n, 2 * PAD, HALF), BF16),
        vmem((16, 2 * occ_rows), F32),
        vmem((n, 16, 2 * occ_rows), F32),
        dma((11,)),
        dma((len(struct_spans(planes)),)),
        dma((GROUPS, n)),
        dma((GROUPS, n)),
        dma((GROUPS, levels)),
        dma((GROUPS, levels)),
        dma((GROUPS, n)),
        dma((GROUPS, n)),
        dma((n,)),
        dma((n,)),
    ]
    return pl.pallas_call(
        kernel,
        out_shape=jax.ShapeDtypeStruct(wave.shape, BF16),
        in_specs=[pl.BlockSpec(memory_space=pl.ANY)] * len(operands),
        out_specs=pl.BlockSpec(memory_space=pltpu.VMEM),
        scratch_shapes=scratch,
        compiler_params=pltpu.CompilerParams(
            collective_id=0, has_side_effects=True, vmem_limit_bytes=56 * 2**20
        ),
        name="perturb",
    )(*operands)


def return_kernel(shift, block, out_ref, send_sem, recv_sem):
    pools = lax.axis_size("pool")
    pool = lax.axis_index("pool")
    ahead = lax.rem(pool + shift, pools)
    behind = lax.rem(pool + pools - shift, pools)
    peers = [ahead] if 2 * shift == pools else [ahead, behind]
    barrier = pltpu.get_barrier_semaphore()
    for peer in peers:
        pl.semaphore_signal(barrier, inc=1, device_id={"pool": peer}, device_id_type=MESH)
    pl.semaphore_wait(barrier, len(peers))
    parts = send_sem.shape[0]
    width = block.shape[-1] // parts
    sent = []
    for i in range(parts):
        span = pl.ds(i * width, width)
        copy = pltpu.make_async_remote_copy(
            src_ref=block.at[:, :, :, span],
            dst_ref=out_ref.at[:, :, :, span],
            send_sem=send_sem.at[i],
            recv_sem=recv_sem.at[i],
            device_id={"pool": behind},
            device_id_type=MESH,
        )
        copy.start()
        sent.append(copy)
    for copy in sent:
        copy.wait()


def give_back(shift, parts, block):
    dma = pltpu.SemaphoreType.DMA
    return pl.pallas_call(
        functools.partial(return_kernel, shift),
        out_shape=jax.ShapeDtypeStruct(block.shape, block.dtype),
        in_specs=[pl.BlockSpec(memory_space=pl.ANY)],
        out_specs=pl.BlockSpec(memory_space=pl.ANY),
        scratch_shapes=[dma((parts,)), dma((parts,))],
        compiler_params=pltpu.CompilerParams(
            collective_id=shift.bit_length(), has_side_effects=True
        ),
        name=f"give_back_{shift}",
    )(block)


RETURN_PARTS = 4


def local(
    wave_block,
    occupied,
    radial,
    k_points,
    g_vectors,
    structure,
    positions,
    displacement,
    coupling,
    atom_kind,
    kq_index,
    occ_count,
):
    pools = lax.axis_size("pool")
    n = lax.axis_size("pw")
    operands = (
        wave_block,
        occupied,
        radial,
        k_points.T,
        g_vectors,
        structure,
        positions,
        displacement,
        coupling.transpose(1, 0, 2),
        atom_kind[None, :],
        kq_index[None, :],
        occ_count[None, :],
    )
    block = perturb(operands, pools, n)
    shifts = [1 << level for level in range((pools - 1).bit_length())]
    branch = 31 - lax.clz(kq_index[0])
    runs = [functools.partial(give_back, shift, RETURN_PARTS) for shift in shifts]
    return lax.switch(branch, runs, block)


def solution(mesh):
    return jax.shard_map(
        local,
        mesh=mesh,
        in_specs=(
            P("pool", None, None, "pw"),
            P("pool", None, None, "pw"),
            P("pool", None, "pw"),
            P(),
            P(None, "pw"),
            P(None, None, "pw"),
            P(),
            P(),
            P(),
            P(),
            P(),
            P(),
        ),
        out_specs=P("pool", None, None, "pw"),
        check_vma=False,
    )
```

profile of v0, /device:TPU:2, one launch (start us, length us, event | category | flops | bytes accessed | tf_op | source)
XLA Modules:
  0.0 56.1 jit_solution(7858581559777355154)
XLA Ops:
  0.7 41.3 %perturb.1 = bf16[1,2,8,7680]{3,2,1,0:T(8,128)(2,1)S(1)} custom-call(bf16[1,2,8,7680]{3,2,1,0:T(8,128)(2,1)} %wave_in.1, bf16[1,2,64,7680]{3,2,1,0:T(8,128)(2,1)} %occ_in.1, bf16[1,9,7680]{2,1,0:T(8,128)(2,1)} %radial_in.1, f32[3,32]{1,0:T(4,128)} %bitcast.8, f32[3,7680]{1,0:T(4,128)} %gvec_in.1, bf16[2,216,7680]{2,1,0:T(8,128)(2,1)} %struct_in.1, ...), custom_call_target="tpu_custom_call" | custom-call | tf_op jit(solution)/shard_map/perturb/pallas_call | solution.py:439
  42.0 13.4 %conditional.1 = (bf16[1,2,8,7680]{3,2,1,0:T(8,128)(2,1)S(1)}) conditional(s32[]{:T(128)} %bitcast, bf16[1,2,8,7680]{3,2,1,0:T(8,128)(2,1)S(1)} %perturb.1, bf16[1,2,8,7680]{3,2,1,0:T(8,128)(2,1)S(1)} %perturb.1, bf16[1,2,8,7680]{3,2,1,0:T(8,128)(2,1)S(1)} %perturb.1, ...), branch_computations={%region_0.0_spmd, %region_1.0_spmd, %region_2.0_spmd, %region_3.0_... | conditional | bytes 8 | solution.py:533
  42.1 13.3 %give_back_16.1 = bf16[1,2,8,7680]{3,2,1,0:T(8,128)(2,1)S(1)} custom-call(bf16[1,2,8,7680]{3,2,1,0:T(8,128)(2,1)S(1)} %block.4), custom_call_target="tpu_custom_call" | custom-call | tf_op jit(solution)/shard_map/cond/branch_4_fun/give_back_16/pallas_call | solution.py:483
  55.4 0.7 %copy.24 = bf16[1,2,8,7680]{3,2,1,0:T(8,128)(2,1)} copy(bf16[1,2,8,7680]{3,2,1,0:T(8,128)(2,1)S(1)} %get-tuple-element.16) | data formatting | bytes 491520
where the time goes:
time: 56.1 us
  Pallas kernels  54.6 us (97%)
  local copies, waits for them, and re-layouts  0.7 us (1%)
  between operations  0.67 us (1%)
    pallas_call x1, Pallas kernels, perturb(): pl.pallas_call(kernel, out_shape=jax.ShapeDtypeStruct(wave.shape, BF16),...  41.3 us
    pallas_call x1, Pallas kernels, give_back(): pl.pallas_call(functools.partial(return_kernel, shift), out_shape=jax.Sha...  13.3 us

commit v1 on v0

--- a/solution.py
+++ b/solution.py
@@ -19,6 +19,13 @@
 MESH = pl.DeviceIdType.MESH
 F32 = jnp.float32
 BF16 = jnp.bfloat16
+
+
+NEAR = ((2, 1), (1, 1), (3, 1), (2, 0), (0, 1), (1, 0), (3, 0))
+
+
+def pw_peer(me, n, step, flip):
+    return lax.rem(me // 2 + step, n // 2) * 2 + (me % 2 + flip) % 2
 
 
 def dot_nt(a, b):
@@ -132,17 +139,13 @@
     )
 
     barrier = pltpu.get_barrier_semaphore()
-    for j in range(1, n):
+    for step, flip in NEAR:
         pl.semaphore_signal(
-            barrier, inc=1, device_id={"pw": lax.rem(me + j, n)}, device_id_type=MESH
+            barrier, inc=1, device_id={"pw": pw_peer(me, n, step, flip)}, device_id_type=MESH
         )
-    offsets = []
-    for level in range(levels):
-        offsets += [o for o in (1 << level, pools - (1 << level)) if o not in offsets]
-    for offset in offsets:
-        pl.semaphore_signal(
-            barrier, inc=1, device_id={"pool": lax.rem(pool + offset, pools)}, device_id_type=MESH
-        )
+    for level in reversed(range(levels)):
+        sender = lax.rem(pool + pools - (1 << level), pools)
+        pl.semaphore_signal(barrier, inc=1, device_id={"pool": sender}, device_id_type=MESH)
 
     for copy in early:
         copy.wait()
@@ -177,8 +180,8 @@
                 raw_im = acc[0, h, im_rows, :] - acc[1, h, re_rows, :]
                 part_send[group, 2 * b + h] = jnp.concatenate([raw_re, raw_im], 0).astype(BF16)
         sent = []
-        for j in range(1, n):
-            peer = lax.rem(me + j, n)
+        for j, (step, flip) in enumerate(NEAR, 1):
+            peer = pw_peer(me, n, step, flip)
             copy = pltpu.make_async_remote_copy(
                 src_ref=part_send.at[group, peer],
                 dst_ref=part_recv.at[group, j],
@@ -198,7 +201,7 @@
             product = dot_nt(moments[0, :, span], struct[c, :, span])
             for h, cols in enumerate(halves):
                 acc[c, h, 0 : 8 * ROWS, 0 : cols.stop - cols.start] += product[:, cols]
-    pl.semaphore_wait(barrier, n - 1 + len(offsets))
+    pl.semaphore_wait(barrier, n - 1 + levels)
     parts = [send_parts(0)]
     fill_moments(1, pl.ds(0, planes))
     for c in range(2):
@@ -274,7 +277,7 @@
             vert[PAD + TYPES * m : PAD + TYPES * (m + 1), :] = (cos_next * im - sin_next * re) * shrink
         vert_send[group] = vert[...].astype(BF16)
         sent = []
-        for level in range(levels):
+        for level in reversed(range(levels)):
             copy = pltpu.make_async_remote_copy(
                 src_ref=vert_send.at[group],
                 dst_ref=candidates.at[group, level],
@@ -295,13 +298,13 @@
             )
         gathered[group, me] = chosen.astype(BF16)
         sent = []
-        for j in range(1, n):
+        for j, (step, flip) in enumerate(NEAR, 1):
             copy = pltpu.make_async_remote_copy(
                 src_ref=gathered.at[group, me],
                 dst_ref=gathered.at[group, me],
                 send_sem=gather_ssem.at[group, j],
                 recv_sem=gather_rsem.at[group, j],
-                device_id={"pw": lax.rem(me + j, n)},
+                device_id={"pw": pw_peer(me, n, step, flip)},
                 device_id_type=MESH,
             )
             copy.start()
@@ -349,13 +352,13 @@
     occ_rows = occ.shape[1]
     corr_send[...] = dot_nt(applied[...].astype(BF16), occ[...].reshape(2 * occ_rows, planes))
     corrs = []
-    for j in range(1, n):
+    for j, (step, flip) in enumerate(NEAR, 1):
         copy = pltpu.make_async_remote_copy(
             src_ref=corr_send,
             dst_ref=corr_recv.at[j],
             send_sem=corr_ssem.at[j],
             recv_sem=corr_rsem.at[j],
-            device_id={"pw": lax.rem(me + j, n)},
+            device_id={"pw": pw_peer(me, n, step, flip)},
             device_id_type=MESH,
         )
         copy.start()
@@ -454,11 +457,9 @@
     pool = lax.axis_index("pool")
     ahead = lax.rem(pool + shift, pools)
     behind = lax.rem(pool + pools - shift, pools)
-    peers = [ahead] if 2 * shift == pools else [ahead, behind]
     barrier = pltpu.get_barrier_semaphore()
-    for peer in peers:
-        pl.semaphore_signal(barrier, inc=1, device_id={"pool": peer}, device_id_type=MESH)
-    pl.semaphore_wait(barrier, len(peers))
+    pl.semaphore_signal(barrier, inc=1, device_id={"pool": ahead}, device_id_type=MESH)
+    pl.semaphore_wait(barrier, 1)
     parts = send_sem.shape[0]
     width = block.shape[-1] // parts
     sent = []

time: 56.1 us -> 55.7 us (level)
    pallas_call x1, Pallas kernels: 41.3 us -> 39.2 us  [perturb(): pl.pallas_call(kernel, out_shape=jax.ShapeDtypeStruct(wave.shape, BF16),...]
    pallas_call x1, Pallas kernels: 13.3 us -> 15.1 us  [give_back(): pl.pallas_call(functools.partial(return_kernel, shift), out_shape=jax.Sha...]
where the time goes in v1:
time: 55.7 us; the launch traced here: 55.6 us
  Pallas kernels  54.2 us (97%)
  local copies, waits for them, and re-layouts  0.7 us (1%)
  between operations  0.67 us (1%)
    pallas_call x1, Pallas kernels, perturb(): pl.pallas_call(kernel, out_shape=jax.ShapeDtypeStruct(wave.shape, BF16),...  39.2 us
    pallas_call x1, Pallas kernels, give_back(): pl.pallas_call(functools.partial(return_kernel, shift), out_shape=jax.Sha...  15.1 us

profile of v1, /device:TPU:2, one launch (start us, length us, event | category | flops | bytes accessed | tf_op | source)
XLA Modules:
  0.0 55.6 jit_solution(16286632116268741659)
XLA Ops:
  0.7 39.2 %perturb.1 = bf16[1,2,8,7680]{3,2,1,0:T(8,128)(2,1)S(1)} custom-call(bf16[1,2,8,7680]{3,2,1,0:T(8,128)(2,1)} %wave_in.1, bf16[1,2,64,7680]{3,2,1,0:T(8,128)(2,1)} %occ_in.1, bf16[1,9,7680]{2,1,0:T(8,128)(2,1)} %radial_in.1, f32[3,32]{1,0:T(4,128)} %bitcast.8, f32[3,7680]{1,0:T(4,128)} %gvec_in.1, bf16[2,216,7680]{2,1,0:T(8,128)(2,1)} %struct_in.1, ...), custom_call_target="tpu_custom_call" | custom-call | tf_op jit(solution)/shard_map/perturb/pallas_call | solution.py:442
  39.8 15.1 %conditional.1 = (bf16[1,2,8,7680]{3,2,1,0:T(8,128)(2,1)S(1)}) conditional(s32[]{:T(128)} %bitcast, bf16[1,2,8,7680]{3,2,1,0:T(8,128)(2,1)S(1)} %perturb.1, bf16[1,2,8,7680]{3,2,1,0:T(8,128)(2,1)S(1)} %perturb.1, bf16[1,2,8,7680]{3,2,1,0:T(8,128)(2,1)S(1)} %perturb.1, ...), branch_computations={%region_0.0_spmd, %region_1.0_spmd, %region_2.0_spmd, %region_3.0_... | conditional | bytes 8 | solution.py:534
  39.9 15.1 %give_back_16.1 = bf16[1,2,8,7680]{3,2,1,0:T(8,128)(2,1)S(1)} custom-call(bf16[1,2,8,7680]{3,2,1,0:T(8,128)(2,1)S(1)} %block.4), custom_call_target="tpu_custom_call" | custom-call | tf_op jit(solution)/shard_map/cond/branch_4_fun/give_back_16/pallas_call | solution.py:484
  54.9 0.7 %copy.24 = bf16[1,2,8,7680]{3,2,1,0:T(8,128)(2,1)} copy(bf16[1,2,8,7680]{3,2,1,0:T(8,128)(2,1)S(1)} %get-tuple-element.16) | data formatting | bytes 491520

commit v2 on v1

--- a/solution.py
+++ b/solution.py
@@ -133,7 +133,6 @@
             (kind_in, kind_raw),
             (index_in, index),
             (count_in, count),
-            (occ_in.at[0], occ),
         ),
         4,
     )
@@ -201,6 +200,7 @@
             product = dot_nt(moments[0, :, span], struct[c, :, span])
             for h, cols in enumerate(halves):
                 acc[c, h, 0 : 8 * ROWS, 0 : cols.stop - cols.start] += product[:, cols]
+    (occ_copy,) = load(((occ_in.at[0], occ),), 10)
     pl.semaphore_wait(barrier, n - 1 + levels)
     parts = [send_parts(0)]
     fill_moments(1, pl.ds(0, planes))
@@ -245,7 +245,8 @@
 
     def send_vertex(group):
         total = part_send[group, me].astype(F32)
-        for j in range(1, n):
+        for j in reversed(range(1, n)):
+            parts[group][j - 1].wait_recv()
             total += part_recv[group, j].astype(F32)
         scale = 1.0 / math.sqrt(PW)
         coef[0] = (cos_here * total[0:PAD] - sin_here * total[PAD:]) * scale
@@ -336,19 +337,21 @@
 
     shifts = []
     for group in range(GROUPS):
-        for copy in parts[group]:
-            copy.wait_recv()
         shifts.append(send_vertex(group))
     passes = []
     for group in range(GROUPS):
         for copy in shifts[group]:
             copy.wait_recv()
         passes.append(pass_vertex(group))
+    for sent in parts + shifts:
+        for copy in sent:
+            copy.wait_send()
     for group in range(GROUPS):
         for copy in passes[group]:
             copy.wait_recv()
         apply_vertex(group)
 
+    occ_copy.wait()
     occ_rows = occ.shape[1]
     corr_send[...] = dot_nt(applied[...].astype(BF16), occ[...].reshape(2 * occ_rows, planes))
     corrs = []
@@ -364,10 +367,12 @@
         copy.start()
         corrs.append(copy)
     live = pick(count[...], pool_lane == pool)
-    for copy in corrs:
-        copy.wait_recv()
+    for sent in passes:
+        for copy in sent:
+            copy.wait_send()
     total = corr_send[...]
-    for j in range(1, n):
+    for j in reversed(range(1, n)):
+        corrs[j - 1].wait_recv()
         total += corr_recv[j]
     row = lax.broadcasted_iota(jnp.int32, total.shape, 0)
     lane = lax.broadcasted_iota(jnp.int32, total.shape, 1)
@@ -380,9 +385,8 @@
     response = (applied[...] - removed).astype(BF16)
     out_ref[0, 0] = response[:8]
     out_ref[0, 1] = response[8:]
-    for sent in parts + shifts + passes + [corrs]:
-        for copy in sent:
-            copy.wait_send()
+    for copy in corrs:
+        copy.wait_send()
 
 
 def struct_spans(planes):

time: 55.7 us -> 49.9 us (0.90); the launches traced: 55.6 us -> 50.8 us
  Pallas kernels: 54.2 us -> 49.3 us
    pallas_call x1, Pallas kernels: 15.1 us -> 10.1 us  [give_back(): pl.pallas_call(functools.partial(return_kernel, shift), out_shape=jax.Sha...]
where the time goes in v2:
time: 49.9 us; the launch traced here: 50.8 us
  Pallas kernels  49.3 us (99%)
  local copies, waits for them, and re-layouts  0.7 us (1%)
  between operations  0.67 us (1%)
    pallas_call x1, Pallas kernels, perturb(): pl.pallas_call(kernel, out_shape=jax.ShapeDtypeStruct(wave.shape, BF16),...  39.3 us
    pallas_call x1, Pallas kernels, give_back(): pl.pallas_call(functools.partial(return_kernel, shift), out_shape=jax.Sha...  10.1 us

profile of v2, /device:TPU:2, one launch (start us, length us, event | category | flops | bytes accessed | tf_op | source)
XLA Modules:
  0.0 50.8 jit_solution(16297599172508415604)
XLA Ops:
  0.7 39.3 %perturb.1 = bf16[1,2,8,7680]{3,2,1,0:T(8,128)(2,1)S(1)} custom-call(bf16[1,2,8,7680]{3,2,1,0:T(8,128)(2,1)} %wave_in.1, bf16[1,2,64,7680]{3,2,1,0:T(8,128)(2,1)} %occ_in.1, bf16[1,9,7680]{2,1,0:T(8,128)(2,1)} %radial_in.1, f32[3,32]{1,0:T(4,128)} %bitcast.8, f32[3,7680]{1,0:T(4,128)} %gvec_in.1, bf16[2,216,7680]{2,1,0:T(8,128)(2,1)} %struct_in.1, ...), custom_call_target="tpu_custom_call" | custom-call | tf_op jit(solution)/shard_map/perturb/pallas_call | solution.py:446
  39.9 10.1 %conditional.1 = (bf16[1,2,8,7680]{3,2,1,0:T(8,128)(2,1)S(1)}) conditional(s32[]{:T(128)} %bitcast, bf16[1,2,8,7680]{3,2,1,0:T(8,128)(2,1)S(1)} %perturb.1, bf16[1,2,8,7680]{3,2,1,0:T(8,128)(2,1)S(1)} %perturb.1, bf16[1,2,8,7680]{3,2,1,0:T(8,128)(2,1)S(1)} %perturb.1, ...), branch_computations={%region_0.0_spmd, %region_1.0_spmd, %region_2.0_spmd, %region_3.0_... | conditional | bytes 8 | solution.py:538
  40.0 10.1 %give_back_8.1 = bf16[1,2,8,7680]{3,2,1,0:T(8,128)(2,1)S(1)} custom-call(bf16[1,2,8,7680]{3,2,1,0:T(8,128)(2,1)S(1)} %block.3), custom_call_target="tpu_custom_call" | custom-call | tf_op jit(solution)/shard_map/cond/branch_3_fun/give_back_8/pallas_call | solution.py:488
  50.1 0.7 %copy.24 = bf16[1,2,8,7680]{3,2,1,0:T(8,128)(2,1)} copy(bf16[1,2,8,7680]{3,2,1,0:T(8,128)(2,1)S(1)} %get-tuple-element.16) | data formatting | bytes 491520
